TPU v7x, 256 devices: a whole 4x4x8 slice. The times are simulated.
256 devices in a mesh: grid: 32 (over x, y, z_lo), orb: 8 (over z_hi, core).
Axes of the slice: x: 4, y: 4, z: 8 (z_hi: 4, z_lo: 2; z = z_hi * 2 + z_lo), core: 2. Of those that a mesh axis runs over, the one named last changes fastest.
Arguments:
- orbitals: float32 [512, 128, 8, 128], P('orb', 'grid'), may hold values from -13 to 13, as said below
- potential: float32 [128, 8, 128], P('grid'), may hold values from -1 to 1
Outputs:
- orthonormal: float32 [512, 128, 8, 128], P('orb', 'grid')
Inputs may be any that keep to these rules, and one draw needn't show every extreme that they name: Trial orbitals, real-valued.
All inputs are finite; a program needn't handle non-finite values.
Results may differ from a plain program's by a relative error of at most 0.0003.
Values sent between devices are 32-bit elements; how exact they have to be, the bound alone decides.
A program may use at most 64 MiB of HBM per device.

v0:
```python
import jax
import jax.numpy as jnp
from jax import lax
from jax.sharding import PartitionSpec as P

lap_weights = (-205.0 / 72.0, 8.0 / 5.0, -1.0 / 5.0, 8.0 / 315.0, -1.0 / 560.0)
lower_edge = 3.0
upper_edge = 11.0


def padded_2(cells, sides, width):
    for axis, dim in sides:
        count = lax.axis_size(axis)
        head = lax.slice_in_dim(cells, 0, width, axis=dim)
        tail = lax.slice_in_dim(cells, cells.shape[dim] - width, cells.shape[dim], axis=dim)
        cells = jnp.concatenate(
            [
                lax.ppermute(tail, axis, [(i, (i + 1) % count) for i in range(count)]),
                cells,
                lax.ppermute(head, axis, [((i + 1) % count, i) for i in range(count)]),
            ],
            axis=dim,
        )
    return cells


def wrap_pad(field, axis_num):
    length = field.shape[axis_num]
    head = lax.slice_in_dim(field, length - 4, length, axis=axis_num)
    tail = lax.slice_in_dim(field, 0, 4, axis=axis_num)
    return jnp.concatenate([head, field, tail], axis=axis_num)


def operate(padded_x, field, potential):
    planes = field.shape[1]
    rows_y = field.shape[2]
    cols_z = field.shape[3]
    padded_yz = wrap_pad(wrap_pad(field, 2), 3)
    laplace = 3.0 * lap_weights[0] * field
    for offset in range(1, 5):
        weight = lap_weights[offset]
        along_x = (
            padded_x[:, 4 + offset : 4 + offset + planes]
            + padded_x[:, 4 - offset : 4 - offset + planes]
        )
        along_y = (
            padded_yz[:, :, 4 + offset : 4 + offset + rows_y, 4 : 4 + cols_z]
            + padded_yz[:, :, 4 - offset : 4 - offset + rows_y, 4 : 4 + cols_z]
        )
        along_z = (
            padded_yz[:, :, 4 : 4 + rows_y, 4 + offset : 4 + offset + cols_z]
            + padded_yz[:, :, 4 : 4 + rows_y, 4 - offset : 4 - offset + cols_z]
        )
        laplace = laplace + weight * (along_x + along_y + along_z)
    return potential[None] * field - 0.5 * laplace


def hamiltonian(field, potential):
    padded = padded_2(field, (("grid", 1),), 4)
    return operate(padded, field, potential)


def filter_with(apply_op, start_field, potential):
    center = 0.5 * (upper_edge + lower_edge)
    half_width = 0.5 * (upper_edge - lower_edge)
    prev_field = start_field
    this_field = (apply_op(start_field, potential) - center * start_field) / half_width
    for degree in range(2):
        next_field = (
            2.0 * (apply_op(this_field, potential) - center * this_field) / half_width - prev_field
        )
        prev_field, this_field = (this_field, next_field)
    return this_field


def per_device(orbitals, potential):
    this_field = filter_with(hamiltonian, orbitals, potential)
    local_orbs = orbitals.shape[0]
    field_shape = this_field.shape
    flat_field = this_field.reshape(local_orbs, -1)
    total_cells = float(flat_field.shape[1] * lax.axis_size("grid"))
    contract = (((1,), (1,)), ((), ()))
    highest = lax.Precision.HIGHEST
    gathered = lax.all_gather(flat_field, "orb", axis=0, tiled=True)
    partial_rows = lax.dot_general(flat_field, gathered, contract, precision=highest)
    summed_rows = lax.psum(partial_rows, "grid")
    margin = lax.all_gather(summed_rows, "orb", axis=0, tiled=True) / total_cells
    factor = jnp.linalg.cholesky(margin)
    identity = jnp.eye(margin.shape[0], dtype=jnp.float32)
    inverse = jax.scipy.linalg.solve_triangular(factor, identity, lower=True)
    first_row = lax.axis_index("orb") * local_orbs
    own_rows = lax.dynamic_slice_in_dim(inverse, first_row, local_orbs, 0)
    rotated = jnp.dot(own_rows, gathered, precision=highest)
    return rotated.reshape(field_shape)


def solution(mesh):
    in_specs = (P("orb", "grid", None, None), P("grid", None, None))
    out_specs = P("orb", "grid", None, None)
    return jax.shard_map(
        per_device, mesh=mesh, in_specs=in_specs, out_specs=out_specs, check_vma=False
    )
```

profile of v0, /device:TPU:1, one launch (start us, length us, event | category | flops | bytes accessed | tf_op | source)
XLA Modules:
  0.0 778.8 jit_solution(14914901883185426809)
XLA Ops:
  17.0 5.1 pad_maximum_fusion
  22.1 13.3 %collective-permute-done.1 = f32[64,4,8,128]{3,2,1,0:T(8,128)S(1)} collective-permute-done((f32[64,4,8,128]{3,2,1,0:T(8,128)}, f32[64,4,8,128]{3,2,1,0:T(8,128)S(1)}, u32[]{:S(2)}, u32[]{:S(2)}) %collective-permute-start.1) | collective-permute-done | bytes 1048608 | tf_op jit(solution)/shard_map/ppermute | solution.py:18
  36.4 18.7 %collective-permute-done = f32[64,4,8,128]{3,2,1,0:T(8,128)S(1)} collective-permute-done((f32[64,4,8,128]{3,2,1,0:T(8,128)}, f32[64,4,8,128]{3,2,1,0:T(8,128)S(1)}, u32[]{:S(2)}, u32[]{:S(2)}) %collective-permute-start) | collective-permute-done | bytes 1048608 | tf_op jit(solution)/shard_map/ppermute | solution.py:20
  56.8 16.4 %broadcast_multiply_fusion.1 = (f32[64,4,8,128]{3,2,1,0:T(8,128)S(1)}, f32[64,4,8,128]{3,2,1,0:T(8,128)}) fusion(f32[64,4,8,128]{3,2,1,0:T(8,128)S(1)} %copy-done, f32[64,4,16,132]{3,2,1,0:T(8,128)} %get-tuple-element.34, f32[64,4,16,132]{3,2,1,0:T(8,128)} %get-tuple-element.33, f32[64,4,4,128]{3,2,1,0:T(4,128)S(1)} %get-tuple-element.43, ...), kind=kLoop, calls=%fused_computation.221 | loop fusion | flops 11272192 | bytes 20987904 | tf_op jit(solution)/shard_map/div | solution.py:67
  84.9 14.2 %collective-permute-done.2 = f32[64,4,8,128]{3,2,1,0:T(8,128)S(1)} collective-permute-done((f32[64,4,8,128]{3,2,1,0:T(8,128)S(1)}, f32[64,4,8,128]{3,2,1,0:T(8,128)S(1)}, u32[]{:S(2)}, u32[]{:S(2)}) %collective-permute-start.2) | collective-permute-done | bytes 1048608 | tf_op jit(solution)/shard_map/ppermute | solution.py:20
  99.0 22.7 %collective-permute-done.3 = f32[64,4,8,128]{3,2,1,0:T(8,128)S(1)} collective-permute-done((f32[64,4,8,128]{3,2,1,0:T(8,128)S(1)}, f32[64,4,8,128]{3,2,1,0:T(8,128)S(1)}, u32[]{:S(2)}, u32[]{:S(2)}) %collective-permute-start.3) | collective-permute-done | bytes 1048608 | tf_op jit(solution)/shard_map/ppermute | solution.py:18
  122.8 18.3 %fusion.33 = f32[64,4,8,128]{3,2,1,0:T(8,128)S(1)} fusion(f32[64,4,8,128]{3,2,1,0:T(8,128)S(1)} %copy-done, f32[64,4,8,128]{3,2,1,0:T(8,128)} %copy-done.13, f32[64,4,8,128]{3,2,1,0:T(8,128)S(1)} %get-tuple-element.21, f32[64,4,8,128]{3,2,1,0:T(8,128)} %copy-done.11, f32[64,4,4,128]{3,2,1,0:T(4,128)} %copy-done.3, f32[64,4,4,128]{3,2,1,0:T(4,128)} %copy-done.2, ...), kind=kLoop, calls=%fused_computation.106 | loop fusion | flops 13107200 | bytes 15745024 | tf_op jit(solution)/shard_map/sub | solution.py:70
  151.4 13.0 %collective-permute-done.4 = f32[64,4,8,128]{3,2,1,0:T(8,128)S(1)} collective-permute-done((f32[64,4,8,128]{3,2,1,0:T(8,128)S(1)}, f32[64,4,8,128]{3,2,1,0:T(8,128)S(1)}, u32[]{:S(2)}, u32[]{:S(2)}) %collective-permute-start.4) | collective-permute-done | bytes 1048608 | tf_op jit(solution)/shard_map/ppermute | solution.py:20
  164.5 23.6 %collective-permute-done.5 = f32[64,4,8,128]{3,2,1,0:T(8,128)S(1)} collective-permute-done((f32[64,4,8,128]{3,2,1,0:T(8,128)S(1)}, f32[64,4,8,128]{3,2,1,0:T(8,128)S(1)}, u32[]{:S(2)}, u32[]{:S(2)}) %collective-permute-start.5) | collective-permute-done | bytes 1048608 | tf_op jit(solution)/shard_map/ppermute | solution.py:18
  189.1 18.1 %fusion.12 = f32[64,4,8,128]{3,2,1,0:T(8,128)S(1)} fusion(f32[64,4,8,128]{3,2,1,0:T(8,128)} %copy-done.14, f32[64,4,8,128]{3,2,1,0:T(8,128)S(1)} %fusion.33, f32[64,4,8,128]{3,2,1,0:T(8,128)} %copy-done.12, f32[64,4,4,128]{3,2,1,0:T(4,128)} %copy-done.5, f32[64,4,4,128]{3,2,1,0:T(4,128)} %copy-done.4, f32[64,4,16,132]{3,2,1,0:T(8,128)} %get-tuple-element.26, ...), kind=kLoop, calls=%fused_computation.85 | loop fusion | flops 13369344 | bytes 14696448 | tf_op jit(solution)/shard_map/sub | solution.py:70
  208.8 80.3 %all-gather.3.cloned.1.call-done = f32[512,4096]{1,0:T(8,128)} async-done(((f32[64,4096]{1,0:T(8,128)}), f32[512,4096]{1,0:T(8,128)}) %all-gather.3.cloned.1.call-update) | async-done | bytes 8388624 | tf_op jit(solution)/shard_map/all_gather | solution.py:84
  289.1 11.3 %fusion.142 = f32[64,512]{1,0:T(8,128)} fusion(f32[512,4096]{1,0:T(8,128)} %all-gather.3.cloned.1.call-done, f32[8,8,32,128]{3,2,1,0:T(8,128)S(1)} %bitcast.61), kind=kOutput, calls=%fused_computation.276 | convolution fusion | flops 1610612736 | bytes 9568256 | tf_op jit(solution)/shard_map/dot_general | solution.py:85
  300.6 276.3 %all-reduce.3.cloned.1.call-done = f32[64,512]{1,0:T(8,128)} async-done(((f32[64,512]{1,0:T(8,128)}), f32[64,512]{1,0:T(8,128)}) %all-reduce.3.cloned.1.call-update) | async-done | bytes 131088 | tf_op jit(solution)/shard_map/psum | solution.py:86
  578.2 41.9 %all-gather.5.cloned.1.call-done = f32[512,512]{1,0:T(8,128)} async-done(((f32[64,512]{1,0:T(8,128)}), f32[512,512]{1,0:T(8,128)}) %all-gather.5.cloned.1.call-update) | async-done | bytes 1048592 | tf_op jit(solution)/shard_map/all_gather | solution.py:87
  622.3 11.7 %cholesky.104 = f32[128,128]{1,0:T(8,128)S(1)} custom-call(f32[128,128]{1,0:T(8,128)S(1)} %cholesky.266), custom_call_target="Cholesky" | custom-call | tf_op jit(solution)/shard_map/jit(cholesky)/cholesky | solution.py:88
  634.2 9.8 %custom-call.31 = f32[1,128,128]{1,2,0:T(8,128)S(1)} custom-call(f32[1,128,128]{2,1,0:T(8,128)S(1)} %get-tuple-element.54), custom_call_target="InvertDiagBlocksLowerTriangular" | custom-call | tf_op jit(solution)/shard_map/jit(cholesky)/cholesky | solution.py:88
  644.7 11.7 %cholesky.217 = f32[128,128]{1,0:T(8,128)S(1)} custom-call(f32[128,128]{1,0:T(8,128)S(1)} %cholesky.270), custom_call_target="Cholesky" | custom-call | tf_op jit(solution)/shard_map/jit(cholesky)/cholesky | solution.py:88
  656.4 10.0 %custom-call.32 = f32[1,128,128]{1,2,0:T(8,128)S(1)} custom-call(f32[1,128,128]{2,1,0:T(8,128)S(1)} %get-tuple-element.51), custom_call_target="InvertDiagBlocksLowerTriangular" | custom-call | tf_op jit(solution)/shard_map/jit(cholesky)/cholesky | solution.py:88
  667.1 12.3 %cholesky.238 = f32[128,128]{1,0:T(8,128)} custom-call(f32[128,128]{1,0:T(8,128)S(1)} %cholesky.275), custom_call_target="Cholesky" | custom-call | tf_op jit(solution)/shard_map/jit(cholesky)/cholesky | solution.py:88
  681.6 11.3 %custom-call.33 = f32[1,128,128]{1,2,0:T(8,128)} custom-call(f32[1,128,128]{2,1,0:T(8,128)} %get-tuple-element.48), custom_call_target="InvertDiagBlocksLowerTriangular" | custom-call | tf_op jit(solution)/shard_map/jit(cholesky)/cholesky | solution.py:88
  694.3 11.9 %cholesky.255 = f32[128,128]{1,0:T(8,128)S(1)} custom-call(f32[128,128]{1,0:T(8,128)S(1)} %convolution_subtract_fusion.5), custom_call_target="Cholesky" | custom-call | tf_op jit(solution)/shard_map/jit(cholesky)/cholesky | solution.py:88
  710.1 9.9 %while.1 = (s32[]{:T(128)}, f32[512,512]{1,0:T(8,128)S(1)}, s32[4,2]{0,1:T(2,128)S(1)}, f32[4,128,128]{2,1,0:T(8,128)}, s32[]{:T(128)}) while((s32[]{:T(128)}, f32[512,512]{1,0:T(8,128)S(1)}, s32[4,2]{0,1:T(2,128)S(1)}, f32[4,128,128]{2,1,0:T(8,128)}, s32[]{:T(128)}) %tuple.38), condition=%wide.while_cond, body=%wide.while_body.sunk | while | flops 2 | bytes 132705 | solution.py:90
  720.0 40.1 %custom-call.34 = f32[4,128,128]{1,2,0:T(8,128)S(1)} custom-call(f32[4,128,128]{2,1,0:T(8,128)} %get-tuple-element.12), custom_call_target="InvertDiagBlocksLowerTriangular" | custom-call | tf_op jit(solution)/shard_map/jit(_solve_triangular)/triangular_solve | solution.py:90
  763.2 7.5 convolution_bitcast_fusion
  (107 shorter events, 62.9 us)
Async XLA Ops:
  6.5 9.2 %copy-start = (f32[64,4,8,128]{3,2,1,0:T(8,128)S(1)}, f32[64,4,8,128]{3,2,1,0:T(8,128)}, u32[]{:S(2)}) copy-start(f32[64,4,8,128]{3,2,1,0:T(8,128)} %param.2) | copy-start | bytes 3145732
  6.5 9.2 %copy-start.15 = (f32[4,8,128]{2,1,0:T(8,128)S(1)}, f32[4,8,128]{2,1,0:T(8,128)}, u32[]{:S(2)}) copy-start(f32[4,8,128]{2,1,0:T(8,128)} %param.3) | copy-start | bytes 49156
  6.5 282.6 %all-gather.3.cloned.1.call-start = ((), (), s32[]{:S(2)}) async-start(), calls=%async_computation | async-start | bytes 9437184 | tf_op jit(solution)/shard_map/all_gather | solution.py:84
  6.5 28.8 %collective-permute-start.1 = (f32[64,4,8,128]{3,2,1,0:T(8,128)}, f32[64,4,8,128]{3,2,1,0:T(8,128)S(1)}, u32[]{:S(2)}, u32[]{:S(2)}) collective-permute-start(f32[64,4,8,128]{3,2,1,0:T(8,128)} %param.2), channel_id=1, source_target_pairs={{0,8},{8,16},{16,24},{24,32},{32,40},{40,48},{48,56},{56,64},{64,7... | collective-permute-start | bytes 3145736 | tf_op jit(solution)/shard_map/ppermute | solution.py:18
  9.0 46.1 %collective-permute-start = (f32[64,4,8,128]{3,2,1,0:T(8,128)}, f32[64,4,8,128]{3,2,1,0:T(8,128)S(1)}, u32[]{:S(2)}, u32[]{:S(2)}) collective-permute-start(f32[64,4,8,128]{3,2,1,0:T(8,128)} %param.2), channel_id=1, source_target_pairs={{8,0},{16,8},{24,16},{32,24},{40,32},{48,40},{56,48},{64,56},{72,6... | collective-permute-start | bytes 3145736 | tf_op jit(solution)/shard_map/ppermute | solution.py:20
  35.4 1.0 copy-start.8
  36.4 18.8 %copy-start.7 = (f32[64,8,8,128]{3,2,1,0:T(8,128)}, f32[64,8,8,128]{3,2,1,0:T(8,128)S(1)}, u32[]{:S(2)}) copy-start(f32[64,8,8,128]{3,2,1,0:T(8,128)S(1)} %get-tuple-element.42) | copy-start | bytes 6291460
  55.2 1.6 copy-start.6
  73.2 25.8 %collective-permute-start.2 = (f32[64,4,8,128]{3,2,1,0:T(8,128)S(1)}, f32[64,4,8,128]{3,2,1,0:T(8,128)S(1)}, u32[]{:S(2)}, u32[]{:S(2)}) collective-permute-start(f32[64,4,8,128]{3,2,1,0:T(8,128)S(1)} %get-tuple-element.21), channel_id=1, source_target_pairs={{8,0},{16,8},{24,16},{32,24},{40,32},{48,40},{56,48},{64,56},{72,6... | collective-permute-start | bytes 3145736 | tf_op jit(solution)/shard_map/ppermute | solution.py:20
  78.1 43.6 %collective-permute-start.3 = (f32[64,4,8,128]{3,2,1,0:T(8,128)S(1)}, f32[64,4,8,128]{3,2,1,0:T(8,128)S(1)}, u32[]{:S(2)}, u32[]{:S(2)}) collective-permute-start(f32[64,4,8,128]{3,2,1,0:T(8,128)S(1)} %get-tuple-element.21), channel_id=1, source_target_pairs={{0,8},{8,16},{16,24},{24,32},{32,40},{40,48},{48,56},{56,64},{64,7... | collective-permute-start | bytes 3145736 | tf_op jit(solution)/shard_map/ppermute | solution.py:18
  78.5 1.3 copy-start.2
  78.5 1.3 copy-start.3
  99.0 22.7 %copy-start.11 = (f32[64,4,8,128]{3,2,1,0:T(8,128)}, f32[64,4,8,128]{3,2,1,0:T(8,128)S(1)}, u32[]{:S(2)}) copy-start(f32[64,4,8,128]{3,2,1,0:T(8,128)S(1)} %collective-permute-done.2) | copy-start | bytes 3145732
  121.7 1.1 copy-start.13
  141.1 23.3 %collective-permute-start.4 = (f32[64,4,8,128]{3,2,1,0:T(8,128)S(1)}, f32[64,4,8,128]{3,2,1,0:T(8,128)S(1)}, u32[]{:S(2)}, u32[]{:S(2)}) collective-permute-start(f32[64,4,8,128]{3,2,1,0:T(8,128)S(1)} %fusion.33), channel_id=1, source_target_pairs={{8,0},{16,8},{24,16},{32,24},{40,32},{48,40},{56,48},{64,56},{72,6... | collective-permute-start | bytes 3145736 | tf_op jit(solution)/shard_map/ppermute | solution.py:20
  144.5 43.5 %collective-permute-start.5 = (f32[64,4,8,128]{3,2,1,0:T(8,128)S(1)}, f32[64,4,8,128]{3,2,1,0:T(8,128)S(1)}, u32[]{:S(2)}, u32[]{:S(2)}) collective-permute-start(f32[64,4,8,128]{3,2,1,0:T(8,128)S(1)} %fusion.33), channel_id=1, source_target_pairs={{0,8},{8,16},{16,24},{24,32},{32,40},{40,48},{48,56},{56,64},{64,7... | collective-permute-start | bytes 3145736 | tf_op jit(solution)/shard_map/ppermute | solution.py:18
  145.1 1.3 copy-start.4
  145.1 1.3 copy-start.5
  146.3 42.8 %copy-start.1 = (f32[64,4,8,128]{3,2,1,0:T(8,128)S(1)}, f32[64,4,8,128]{3,2,1,0:T(8,128)}, u32[]{:S(2)}) copy-start(f32[64,4,8,128]{3,2,1,0:T(8,128)} %get-tuple-element.22) | copy-start | bytes 3145732
  164.5 23.6 %copy-start.12 = (f32[64,4,8,128]{3,2,1,0:T(8,128)}, f32[64,4,8,128]{3,2,1,0:T(8,128)S(1)}, u32[]{:S(2)}) copy-start(f32[64,4,8,128]{3,2,1,0:T(8,128)S(1)} %collective-permute-done.4) | copy-start | bytes 3145732
  188.0 1.1 copy-start.14
  208.8 368.2 %all-reduce.3.cloned.1.call-start = ((), (), s32[]{:S(2)}) async-start(), calls=%async_computation.1 | async-start | bytes 262144 | tf_op jit(solution)/shard_map/psum | solution.py:86
  300.4 319.7 %all-gather.5.cloned.1.call-start = ((), (), s32[]{:S(2)}) async-start(), calls=%async_computation.2 | async-start | bytes 1179648 | tf_op jit(solution)/shard_map/all_gather | solution.py:87
  679.4 81.0 %copy-start.10 = (f32[512,512]{1,0:T(8,128)S(1)}, f32[512,512]{1,0:T(8,128)}, u32[]{:S(2)}) copy-start(f32[512,512]{1,0:T(8,128)} %fusion.114) | copy-start | bytes 3145732
  (1 other events, 1.0 us)
Sparse Core Ops, SparseCore 0:
  208.9 80.1 all-gather.2
  300.5 276.3 all-reduce.2
  579.0 41.0 all-gather.4
where the time goes:
time: 786 us; the launch traced here: 779 us
  waiting for transfers between devices  504 us (64%)
  other arithmetic  193 us (25%)
  matrix products  24.5 us (3%)
  local copies, waits for them, and re-layouts  24.2 us (3%)
  between operations  16.5 us (2%)
  starting transfers between devices  16.3 us (2%)
    psum x1, waiting for transfers between devices, per_device(): summed_rows = lax.psum(partial_rows, 'grid')  276 us
    another operation x14, other arithmetic, per_device(): factor = jnp.linalg.cholesky(margin)  82.3 us
    all_gather x1, waiting for transfers between devices, per_device(): gathered = lax.all_gather(flat_field, 'orb', axis=0, tiled=True)  80.3 us
    ppermute x3, waiting for transfers between devices, padded_2(): lax.ppermute(tail, axis, [(i, (i + 1) % count) for i in range(count)])  59.6 us
    ppermute x3, waiting for transfers between devices, padded_2(): lax.ppermute(head, axis, [((i + 1) % count, i) for i in range(count)])  45.9 us
    all_gather x1, waiting for transfers between devices, per_device(): lax.all_gather(summed_rows, 'orb', axis=0, tiled=True) / total_cells  41.9 us
    another operation x3, other arithmetic, per_device(): inverse = jax.scipy.linalg.solve_triangular(factor, identity, lower=True)  40.3 us
    sub x2, other arithmetic, filter_with(): 2.0 * (apply_op(this_field, potential) - center * this_field) / half_width  36.4 us
  transfers between devices with their start and end apart: 9, of which 9 were waited for; matrix products, arithmetic and copies ran while one was open for 3% of the time, Pallas kernels for 0%

commit v1 on v0

--- a/solution.py
+++ b/solution.py
@@ -83,7 +83,7 @@
     highest = lax.Precision.HIGHEST
     gathered = lax.all_gather(flat_field, "orb", axis=0, tiled=True)
     partial_rows = lax.dot_general(flat_field, gathered, contract, precision=highest)
-    summed_rows = lax.psum(partial_rows, "grid")
+    summed_rows = jnp.sum(lax.all_gather(partial_rows, "grid"), axis=0)
     margin = lax.all_gather(summed_rows, "orb", axis=0, tiled=True) / total_cells
     factor = jnp.linalg.cholesky(margin)
     identity = jnp.eye(margin.shape[0], dtype=jnp.float32)

time: 786 us -> 675 us (0.86)
  waiting for transfers between devices: 504 us -> 390 us
    psum x1 -> x0, waiting for transfers between devices: 276 us -> none  [per_device(): summed_rows = lax.psum(partial_rows, 'grid')]
    all_gather x0 -> x1, waiting for transfers between devices: none -> 154 us  [per_device(): summed_rows = jnp.sum(lax.all_gather(partial_rows, 'grid'), axis=0)]
    all_gather x1, waiting for transfers between devices: 41.9 us -> 49.8 us  [per_device(): lax.all_gather(summed_rows, 'orb', axis=0, tiled=True) / total_cells]
where the time goes in v1:
time: 675 us; the launch traced here: 668 us
  waiting for transfers between devices  390 us (58%)
  other arithmetic  197 us (29%)
  matrix products  24.5 us (4%)
  local copies, waits for them, and re-layouts  24.4 us (4%)
  between operations  16.5 us (2%)
  starting transfers between devices  16.3 us (2%)
    all_gather x1, waiting for transfers between devices, per_device(): summed_rows = jnp.sum(lax.all_gather(partial_rows, 'grid'), axis=0)  154 us
    another operation x14, other arithmetic, per_device(): factor = jnp.linalg.cholesky(margin)  82.5 us
    all_gather x1, waiting for transfers between devices, per_device(): gathered = lax.all_gather(flat_field, 'orb', axis=0, tiled=True)  80.3 us
    ppermute x3, waiting for transfers between devices, padded_2(): lax.ppermute(tail, axis, [(i, (i + 1) % count) for i in range(count)])  59.6 us
    all_gather x1, waiting for transfers between devices, per_device(): lax.all_gather(summed_rows, 'orb', axis=0, tiled=True) / total_cells  49.8 us
    ppermute x3, waiting for transfers between devices, padded_2(): lax.ppermute(head, axis, [((i + 1) % count, i) for i in range(count)])  45.9 us
    another operation x3, other arithmetic, per_device(): inverse = jax.scipy.linalg.solve_triangular(factor, identity, lower=True)  40.3 us
    sub x2, other arithmetic, filter_with(): 2.0 * (apply_op(this_field, potential) - center * this_field) / half_width  36.4 us
  transfers between devices with their start and end apart: 9, of which 9 were waited for; matrix products, arithmetic and copies ran while one was open for 3% of the time, Pallas kernels for 0%

profile of v1, /device:TPU:1, one launch (start us, length us, event | category | flops | bytes accessed | tf_op | source)
XLA Modules:
  0.0 668.3 jit_solution(6503975726402582195)
XLA Ops:
  17.0 5.1 pad_maximum_fusion
  22.1 13.3 %collective-permute-done.1 = f32[64,4,8,128]{3,2,1,0:T(8,128)S(1)} collective-permute-done((f32[64,4,8,128]{3,2,1,0:T(8,128)}, f32[64,4,8,128]{3,2,1,0:T(8,128)S(1)}, u32[]{:S(2)}, u32[]{:S(2)}) %collective-permute-start.1) | collective-permute-done | bytes 1048608 | tf_op jit(solution)/shard_map/ppermute | solution.py:18
  36.4 18.7 %collective-permute-done = f32[64,4,8,128]{3,2,1,0:T(8,128)S(1)} collective-permute-done((f32[64,4,8,128]{3,2,1,0:T(8,128)}, f32[64,4,8,128]{3,2,1,0:T(8,128)S(1)}, u32[]{:S(2)}, u32[]{:S(2)}) %collective-permute-start) | collective-permute-done | bytes 1048608 | tf_op jit(solution)/shard_map/ppermute | solution.py:20
  56.8 16.4 %broadcast_multiply_fusion.1 = (f32[64,4,8,128]{3,2,1,0:T(8,128)S(1)}, f32[64,4,8,128]{3,2,1,0:T(8,128)}) fusion(f32[64,4,8,128]{3,2,1,0:T(8,128)S(1)} %copy-done, f32[64,4,16,132]{3,2,1,0:T(8,128)} %get-tuple-element.34, f32[64,4,16,132]{3,2,1,0:T(8,128)} %get-tuple-element.33, f32[64,4,4,128]{3,2,1,0:T(4,128)S(1)} %get-tuple-element.43, ...), kind=kLoop, calls=%fused_computation.221 | loop fusion | flops 11272192 | bytes 20987904 | tf_op jit(solution)/shard_map/div | solution.py:67
  84.9 14.2 %collective-permute-done.2 = f32[64,4,8,128]{3,2,1,0:T(8,128)S(1)} collective-permute-done((f32[64,4,8,128]{3,2,1,0:T(8,128)S(1)}, f32[64,4,8,128]{3,2,1,0:T(8,128)S(1)}, u32[]{:S(2)}, u32[]{:S(2)}) %collective-permute-start.2) | collective-permute-done | bytes 1048608 | tf_op jit(solution)/shard_map/ppermute | solution.py:20
  99.0 22.7 %collective-permute-done.3 = f32[64,4,8,128]{3,2,1,0:T(8,128)S(1)} collective-permute-done((f32[64,4,8,128]{3,2,1,0:T(8,128)S(1)}, f32[64,4,8,128]{3,2,1,0:T(8,128)S(1)}, u32[]{:S(2)}, u32[]{:S(2)}) %collective-permute-start.3) | collective-permute-done | bytes 1048608 | tf_op jit(solution)/shard_map/ppermute | solution.py:18
  122.8 18.3 %fusion.33 = f32[64,4,8,128]{3,2,1,0:T(8,128)S(1)} fusion(f32[64,4,8,128]{3,2,1,0:T(8,128)S(1)} %copy-done, f32[64,4,8,128]{3,2,1,0:T(8,128)} %copy-done.13, f32[64,4,8,128]{3,2,1,0:T(8,128)S(1)} %get-tuple-element.21, f32[64,4,8,128]{3,2,1,0:T(8,128)} %copy-done.11, f32[64,4,4,128]{3,2,1,0:T(4,128)} %copy-done.3, f32[64,4,4,128]{3,2,1,0:T(4,128)} %copy-done.2, ...), kind=kLoop, calls=%fused_computation.106 | loop fusion | flops 13107200 | bytes 15745024 | tf_op jit(solution)/shard_map/sub | solution.py:70
  151.4 13.0 %collective-permute-done.4 = f32[64,4,8,128]{3,2,1,0:T(8,128)S(1)} collective-permute-done((f32[64,4,8,128]{3,2,1,0:T(8,128)S(1)}, f32[64,4,8,128]{3,2,1,0:T(8,128)S(1)}, u32[]{:S(2)}, u32[]{:S(2)}) %collective-permute-start.4) | collective-permute-done | bytes 1048608 | tf_op jit(solution)/shard_map/ppermute | solution.py:20
  164.5 23.6 %collective-permute-done.5 = f32[64,4,8,128]{3,2,1,0:T(8,128)S(1)} collective-permute-done((f32[64,4,8,128]{3,2,1,0:T(8,128)S(1)}, f32[64,4,8,128]{3,2,1,0:T(8,128)S(1)}, u32[]{:S(2)}, u32[]{:S(2)}) %collective-permute-start.5) | collective-permute-done | bytes 1048608 | tf_op jit(solution)/shard_map/ppermute | solution.py:18
  189.1 18.1 %fusion.12 = f32[64,4,8,128]{3,2,1,0:T(8,128)S(1)} fusion(f32[64,4,8,128]{3,2,1,0:T(8,128)} %copy-done.14, f32[64,4,8,128]{3,2,1,0:T(8,128)S(1)} %fusion.33, f32[64,4,8,128]{3,2,1,0:T(8,128)} %copy-done.12, f32[64,4,4,128]{3,2,1,0:T(4,128)} %copy-done.5, f32[64,4,4,128]{3,2,1,0:T(4,128)} %copy-done.4, f32[64,4,16,132]{3,2,1,0:T(8,128)} %get-tuple-element.26, ...), kind=kLoop, calls=%fused_computation.85 | loop fusion | flops 13369344 | bytes 14696448 | tf_op jit(solution)/shard_map/sub | solution.py:70
  208.8 80.3 %all-gather.5.cloned.1.call-done = f32[512,4096]{1,0:T(8,128)} async-done(((f32[64,4096]{1,0:T(8,128)}), f32[512,4096]{1,0:T(8,128)}) %all-gather.5.cloned.1.call-update) | async-done | bytes 8388624 | tf_op jit(solution)/shard_map/all_gather | solution.py:84
  289.1 11.3 %fusion.142 = f32[64,512]{1,0:T(8,128)} fusion(f32[512,4096]{1,0:T(8,128)} %all-gather.5.cloned.1.call-done, f32[8,8,32,128]{3,2,1,0:T(8,128)S(1)} %bitcast.62), kind=kOutput, calls=%fused_computation.276 | convolution fusion | flops 1610612736 | bytes 9568256 | tf_op jit(solution)/shard_map/dot_general | solution.py:85
  300.6 154.3 %all-gather.9.cloned.1.call-done = f32[2048,512]{1,0:T(8,128)} async-done(((f32[64,512]{1,0:T(8,128)}), f32[2048,512]{1,0:T(8,128)}) %all-gather.9.cloned.1.call-update) | async-done | bytes 4194320 | tf_op jit(solution)/shard_map/all_gather | solution.py:86
  459.3 49.8 %all-gather.7.cloned.1.call-done = f32[512,512]{1,0:T(8,128)} async-done(((f32[64,512]{1,0:T(8,128)}), f32[512,512]{1,0:T(8,128)}) %all-gather.7.cloned.1.call-update) | async-done | bytes 1048592 | tf_op jit(solution)/shard_map/all_gather | solution.py:87
  511.4 11.7 %cholesky.104 = f32[128,128]{1,0:T(8,128)S(1)} custom-call(f32[128,128]{1,0:T(8,128)S(1)} %cholesky.266), custom_call_target="Cholesky" | custom-call | tf_op jit(solution)/shard_map/jit(cholesky)/cholesky | solution.py:88
  523.2 9.8 %custom-call.31 = f32[1,128,128]{1,2,0:T(8,128)S(1)} custom-call(f32[1,128,128]{2,1,0:T(8,128)S(1)} %get-tuple-element.54), custom_call_target="InvertDiagBlocksLowerTriangular" | custom-call | tf_op jit(solution)/shard_map/jit(cholesky)/cholesky | solution.py:88
  533.7 11.7 %cholesky.217 = f32[128,128]{1,0:T(8,128)S(1)} custom-call(f32[128,128]{1,0:T(8,128)S(1)} %cholesky.270), custom_call_target="Cholesky" | custom-call | tf_op jit(solution)/shard_map/jit(cholesky)/cholesky | solution.py:88
  545.5 10.0 %custom-call.32 = f32[1,128,128]{1,2,0:T(8,128)S(1)} custom-call(f32[1,128,128]{2,1,0:T(8,128)S(1)} %get-tuple-element.51), custom_call_target="InvertDiagBlocksLowerTriangular" | custom-call | tf_op jit(solution)/shard_map/jit(cholesky)/cholesky | solution.py:88
  556.1 12.3 %cholesky.238 = f32[128,128]{1,0:T(8,128)} custom-call(f32[128,128]{1,0:T(8,128)S(1)} %cholesky.275), custom_call_target="Cholesky" | custom-call | tf_op jit(solution)/shard_map/jit(cholesky)/cholesky | solution.py:88
  570.7 11.3 %custom-call.33 = f32[1,128,128]{1,2,0:T(8,128)} custom-call(f32[1,128,128]{2,1,0:T(8,128)} %get-tuple-element.48), custom_call_target="InvertDiagBlocksLowerTriangular" | custom-call | tf_op jit(solution)/shard_map/jit(cholesky)/cholesky | solution.py:88
  583.4 12.0 %cholesky.255 = f32[128,128]{1,0:T(8,128)S(1)} custom-call(f32[128,128]{1,0:T(8,128)S(1)} %convolution_subtract_fusion.5), custom_call_target="Cholesky" | custom-call | tf_op jit(solution)/shard_map/jit(cholesky)/cholesky | solution.py:88
  599.3 10.1 %while.1 = (s32[]{:T(128)}, f32[512,512]{1,0:T(8,128)S(1)}, s32[4,2]{0,1:T(2,128)S(1)}, f32[4,128,128]{2,1,0:T(8,128)}, s32[]{:T(128)}) while((s32[]{:T(128)}, f32[512,512]{1,0:T(8,128)S(1)}, s32[4,2]{0,1:T(2,128)S(1)}, f32[4,128,128]{2,1,0:T(8,128)}, s32[]{:T(128)}) %tuple.38), condition=%wide.while_cond, body=%wide.while_body.sunk | while | flops 2 | bytes 132705 | solution.py:90
  609.4 40.1 %custom-call.34 = f32[4,128,128]{1,2,0:T(8,128)S(1)} custom-call(f32[4,128,128]{2,1,0:T(8,128)} %get-tuple-element.12), custom_call_target="InvertDiagBlocksLowerTriangular" | custom-call | tf_op jit(solution)/shard_map/jit(_solve_triangular)/triangular_solve | solution.py:90
  652.6 7.5 %convolution_bitcast_fusion = f32[8,8,32,128]{3,1,2,0:T(8,128)S(1)} fusion(f32[512,4096]{1,0:T(8,128)} %all-gather.5.cloned.1.call-done, s32[]{:T(128)S(6)} %select_n.8, f32[128,512]{1,0:T(8,128)S(1)} %fusion.116, f32[128,512]{1,0:T(8,128)S(1)} %fusion.132, f32[128,512]{1,0:T(8,128)S(1)} %fusion.130, f32[128,512]{1,0:T(8,128)S(1)} %fusion.129), kind=kOutput, calls=%fused_computation.63 | convolution fusion | flops 1610711040 | bytes 10485764 | tf_op jit(solution)/shard_map/dot_general | solution.py:93
  (108 shorter events, 66.3 us)
Async XLA Ops:
  6.5 9.2 %copy-start = (f32[64,4,8,128]{3,2,1,0:T(8,128)S(1)}, f32[64,4,8,128]{3,2,1,0:T(8,128)}, u32[]{:S(2)}) copy-start(f32[64,4,8,128]{3,2,1,0:T(8,128)} %param.2) | copy-start | bytes 3145732
  6.5 9.2 %copy-start.15 = (f32[4,8,128]{2,1,0:T(8,128)S(1)}, f32[4,8,128]{2,1,0:T(8,128)}, u32[]{:S(2)}) copy-start(f32[4,8,128]{2,1,0:T(8,128)} %param.3) | copy-start | bytes 49156
  6.5 282.6 %all-gather.5.cloned.1.call-start = ((), (), s32[]{:S(2)}) async-start(), calls=%async_computation | async-start | bytes 9437184 | tf_op jit(solution)/shard_map/all_gather | solution.py:84
  6.5 28.8 %collective-permute-start.1 = (f32[64,4,8,128]{3,2,1,0:T(8,128)}, f32[64,4,8,128]{3,2,1,0:T(8,128)S(1)}, u32[]{:S(2)}, u32[]{:S(2)}) collective-permute-start(f32[64,4,8,128]{3,2,1,0:T(8,128)} %param.2), channel_id=1, source_target_pairs={{0,8},{8,16},{16,24},{24,32},{32,40},{40,48},{48,56},{56,64},{64,7... | collective-permute-start | bytes 3145736 | tf_op jit(solution)/shard_map/ppermute | solution.py:18
  9.0 46.1 %collective-permute-start = (f32[64,4,8,128]{3,2,1,0:T(8,128)}, f32[64,4,8,128]{3,2,1,0:T(8,128)S(1)}, u32[]{:S(2)}, u32[]{:S(2)}) collective-permute-start(f32[64,4,8,128]{3,2,1,0:T(8,128)} %param.2), channel_id=1, source_target_pairs={{8,0},{16,8},{24,16},{32,24},{40,32},{48,40},{56,48},{64,56},{72,6... | collective-permute-start | bytes 3145736 | tf_op jit(solution)/shard_map/ppermute | solution.py:20
  35.4 1.0 copy-start.8
  36.4 18.8 %copy-start.7 = (f32[64,8,8,128]{3,2,1,0:T(8,128)}, f32[64,8,8,128]{3,2,1,0:T(8,128)S(1)}, u32[]{:S(2)}) copy-start(f32[64,8,8,128]{3,2,1,0:T(8,128)S(1)} %get-tuple-element.42) | copy-start | bytes 6291460
  55.2 1.6 copy-start.6
  73.2 25.8 %collective-permute-start.2 = (f32[64,4,8,128]{3,2,1,0:T(8,128)S(1)}, f32[64,4,8,128]{3,2,1,0:T(8,128)S(1)}, u32[]{:S(2)}, u32[]{:S(2)}) collective-permute-start(f32[64,4,8,128]{3,2,1,0:T(8,128)S(1)} %get-tuple-element.21), channel_id=1, source_target_pairs={{8,0},{16,8},{24,16},{32,24},{40,32},{48,40},{56,48},{64,56},{72,6... | collective-permute-start | bytes 3145736 | tf_op jit(solution)/shard_map/ppermute | solution.py:20
  78.1 43.6 %collective-permute-start.3 = (f32[64,4,8,128]{3,2,1,0:T(8,128)S(1)}, f32[64,4,8,128]{3,2,1,0:T(8,128)S(1)}, u32[]{:S(2)}, u32[]{:S(2)}) collective-permute-start(f32[64,4,8,128]{3,2,1,0:T(8,128)S(1)} %get-tuple-element.21), channel_id=1, source_target_pairs={{0,8},{8,16},{16,24},{24,32},{32,40},{40,48},{48,56},{56,64},{64,7... | collective-permute-start | bytes 3145736 | tf_op jit(solution)/shard_map/ppermute | solution.py:18
  78.5 1.3 copy-start.2
  78.5 1.3 copy-start.3
  99.0 22.7 %copy-start.11 = (f32[64,4,8,128]{3,2,1,0:T(8,128)}, f32[64,4,8,128]{3,2,1,0:T(8,128)S(1)}, u32[]{:S(2)}) copy-start(f32[64,4,8,128]{3,2,1,0:T(8,128)S(1)} %collective-permute-done.2) | copy-start | bytes 3145732
  121.7 1.1 copy-start.13
  141.1 23.3 %collective-permute-start.4 = (f32[64,4,8,128]{3,2,1,0:T(8,128)S(1)}, f32[64,4,8,128]{3,2,1,0:T(8,128)S(1)}, u32[]{:S(2)}, u32[]{:S(2)}) collective-permute-start(f32[64,4,8,128]{3,2,1,0:T(8,128)S(1)} %fusion.33), channel_id=1, source_target_pairs={{8,0},{16,8},{24,16},{32,24},{40,32},{48,40},{56,48},{64,56},{72,6... | collective-permute-start | bytes 3145736 | tf_op jit(solution)/shard_map/ppermute | solution.py:20
  144.5 43.5 %collective-permute-start.5 = (f32[64,4,8,128]{3,2,1,0:T(8,128)S(1)}, f32[64,4,8,128]{3,2,1,0:T(8,128)S(1)}, u32[]{:S(2)}, u32[]{:S(2)}) collective-permute-start(f32[64,4,8,128]{3,2,1,0:T(8,128)S(1)} %fusion.33), channel_id=1, source_target_pairs={{0,8},{8,16},{16,24},{24,32},{32,40},{40,48},{48,56},{56,64},{64,7... | collective-permute-start | bytes 3145736 | tf_op jit(solution)/shard_map/ppermute | solution.py:18
  145.1 1.3 copy-start.4
  145.1 1.3 copy-start.5
  146.3 42.8 %copy-start.1 = (f32[64,4,8,128]{3,2,1,0:T(8,128)S(1)}, f32[64,4,8,128]{3,2,1,0:T(8,128)}, u32[]{:S(2)}) copy-start(f32[64,4,8,128]{3,2,1,0:T(8,128)} %get-tuple-element.22) | copy-start | bytes 3145732
  164.5 23.6 %copy-start.12 = (f32[64,4,8,128]{3,2,1,0:T(8,128)}, f32[64,4,8,128]{3,2,1,0:T(8,128)S(1)}, u32[]{:S(2)}) copy-start(f32[64,4,8,128]{3,2,1,0:T(8,128)S(1)} %collective-permute-done.4) | copy-start | bytes 3145732
  188.0 1.1 copy-start.14
  208.8 246.1 %all-gather.9.cloned.1.call-start = ((), (), s32[]{:S(2)}) async-start(), calls=%async_computation.2 | async-start | bytes 4325376 | tf_op jit(solution)/shard_map/all_gather | solution.py:86
  300.4 208.7 %all-gather.7.cloned.1.call-start = ((), (), s32[]{:S(2)}) async-start(), calls=%async_computation.1 | async-start | bytes 1179648 | tf_op jit(solution)/shard_map/all_gather | solution.py:87
  568.5 81.4 %copy-start.10 = (f32[512,512]{1,0:T(8,128)S(1)}, f32[512,512]{1,0:T(8,128)}, u32[]{:S(2)}) copy-start(f32[512,512]{1,0:T(8,128)} %fusion.114) | copy-start | bytes 3145732
  (1 other events, 1.0 us)
Sparse Core Ops, SparseCore 0:
  208.9 80.1 all-gather.4
  300.5 154.3 all-gather.8
  458.2 50.8 all-gather.6
